TPU v7x, 32 devices: a whole 2x2x4 slice. The times are simulated.
32 devices in a mesh: dp: 4 (over z), expert: 8 (over y, x, core).
Axes of the slice: x: 2, y: 2, z: 4, core: 2. Of those that a mesh axis runs over, the one named last changes fastest.
Arguments:
- tokens: bfloat16 [4096, 2880], P(('expert', 'dp')), may hold values from -6 to 6
- passes_through: int32 [4096], P(('expert', 'dp')), may hold values from 0 to 1, as said below
- keep_weight: float32 [4096], P(('expert', 'dp')), may hold values from 0.25 to 2
- norm_gain: float32 [2880], replicated, may hold values from 0.5 to 1.5
- routes: int32 [8, 32, 4], P('expert'), may hold values from 0 to 7, all different within a row; in each aligned block of 32 rows (0 to 31, 32 to 63, ..., all dimensions but the last counted through in order) at most 20 rows name the same one
- gate_values: float32 [8, 32, 4], P('expert'), may hold values from 0.05 to 1
- w_gate: bfloat16 [8, 2880, 2880], P('expert', None, 'dp'), may hold values from -0.109375 to 0.109375
- w_up: bfloat16 [8, 2880, 2880], P('expert', None, 'dp'), may hold values from -0.109375 to 0.109375
- w_down: bfloat16 [8, 2880, 2880], P('expert', 'dp'), may hold values from -0.109375 to 0.109375
Outputs:
- mixed: bfloat16 [4096, 2880], P(('expert', 'dp'))
Inputs may be any that keep to these rules, and one draw needn't show every extreme that they name: `passes_through`: each sequence of 512 tokens has exactly 32 survivors. The 128 tokens of one index of dp hold at most 24 survivors, and in every sequence one such group holds exactly 24. `routes`: the 4 ids of a survivor differ. Within one sequence no expert is named more than 20 times, a bound that some block reaches.
All inputs are finite; a program needn't handle non-finite values.
Results may differ from a plain program's by a relative error of at most 0.005.
Values may be sent and summed in bfloat16 or wider, within the bound.
A program may use at most 64 MiB of HBM per device.

v0:
```python
import jax
import jax.numpy as jnp
from jax import lax
from jax.sharding import PartitionSpec as P


def rescaled_entries(rows_in, gain_row):
    scaling = lax.rsqrt(jnp.mean(rows_in * rows_in, axis=-1, keepdims=True) + 1e-05)
    return (rows_in * scaling * gain_row).astype(jnp.bfloat16)


def local(
    tokens, passes_through, keep_weight, norm_gain, routes, gate_values, w_gate, w_up, w_down
):
    piece_vectors, feature_width = tokens.shape
    batch_clusters = lax.axis_size("dp")
    experts = lax.axis_size("expert")
    most_local = 3 * (piece_vectors // 16)
    seq_keep = routes.shape[1]
    top_count = routes.shape[2]
    capacity = max(2, batch_clusters * (piece_vectors // 16) * top_count // experts * 5 // 4)
    ranking = jnp.cumsum(passes_through) - 1
    picker = (
        (ranking[None, :] == jnp.arange(most_local)[:, None]) & (passes_through[None, :] == 1)
    ).astype(jnp.bfloat16)
    compact = jnp.dot(picker, tokens, preferred_element_type=jnp.float32)
    normalized_rows = rescaled_entries(compact, norm_gain)
    remaining_total = jnp.sum(passes_through)
    gathered, counts_all = (
        lax.all_gather(normalized_rows, "dp", axis=0, tiled=True),
        lax.all_gather(remaining_total.reshape(1), "dp", axis=0, tiled=True),
    )
    offsets = jnp.cumsum(counts_all) - counts_all
    within = jnp.arange(most_local, dtype=jnp.int32)
    token_positions = (offsets[:, None] + within[None, :]).reshape(-1)
    valid_mask = (within[None, :] < counts_all[:, None]).reshape(-1)
    order_pick = (
        (token_positions[None, :] == jnp.arange(seq_keep)[:, None]) & valid_mask[None, :]
    ).astype(jnp.bfloat16)
    column_rows = jnp.dot(order_pick, gathered, preferred_element_type=jnp.float32).astype(
        jnp.bfloat16
    )
    flat_routes = routes.reshape(-1)
    onehot = (flat_routes[:, None] == jnp.arange(experts)[None, :]).astype(jnp.int32)
    slot_rank = jnp.sum((jnp.cumsum(onehot, axis=0) - onehot) * onehot, axis=1)
    targets = (flat_routes * capacity + slot_rank).reshape(seq_keep, top_count)
    slot_ids = jnp.arange(experts * capacity)
    dispatch = jnp.any(targets[None, :, :] == slot_ids[:, None, None], axis=-1).astype(jnp.bfloat16)
    buffer = jnp.dot(dispatch, column_rows, preferred_element_type=jnp.float32).astype(jnp.bfloat16)
    received = lax.all_to_all(buffer, "expert", split_axis=0, concat_axis=0, tiled=True)
    gate_proj = jnp.dot(received, w_gate[0], preferred_element_type=jnp.float32)
    up_proj = jnp.dot(received, w_up[0], preferred_element_type=jnp.float32)
    hidden = ((up_proj + 1.0) * gate_proj * jax.nn.sigmoid(1.702 * gate_proj)).astype(jnp.bfloat16)
    partials = jnp.dot(hidden, w_down[0], preferred_element_type=jnp.float32)
    summed = lax.psum_scatter(partials.astype(jnp.bfloat16), "dp", scatter_dimension=1, tiled=True)
    returned = lax.all_to_all(summed, "expert", split_axis=0, concat_axis=0, tiled=True)
    combine_weights = jnp.sum(
        (targets[:, :, None] == slot_ids[None, None, :]).astype(jnp.float32)
        * gate_values[0][:, :, None],
        axis=1,
    )
    mixture = jnp.dot(
        combine_weights, returned.astype(jnp.float32), precision=lax.Precision.HIGHEST
    )
    moe_rows = mixture.astype(jnp.bfloat16)
    owned = jnp.dot(order_pick.T, moe_rows, preferred_element_type=jnp.float32).astype(jnp.bfloat16)
    own_rows = lax.all_to_all(owned, "dp", split_axis=0, concat_axis=1, tiled=True)
    spread = jnp.dot(picker.T, own_rows, preferred_element_type=jnp.float32)
    result = tokens.astype(jnp.float32) + keep_weight[:, None] * spread
    return result.astype(jnp.bfloat16)


def solution(mesh):
    return jax.shard_map(
        local,
        mesh=mesh,
        in_specs=(
            P(("expert", "dp"), None),
            P(("expert", "dp")),
            P(("expert", "dp")),
            P(),
            P("expert", None, None),
            P("expert", None, None),
            P("expert", None, "dp"),
            P("expert", None, "dp"),
            P("expert", "dp", None),
        ),
        out_specs=P(("expert", "dp"), None),
        check_vma=False,
    )
```

profile of v0, /device:TPU:0, one launch (start us, length us, event | category | flops | bytes accessed | tf_op | source)
XLA Modules:
  0.0 139.1 jit_solution(5159658834341961589)
XLA Ops:
  6.5 0.7 broadcast_compare_fusion
  7.2 0.8 copy.46
  8.0 1.3 reduce_sum.40
  9.2 0.2 reduce-window.17
  9.5 1.5 %multiply_reduce_fusion = (f32[24]{0:T(128)S(1)}, f32[24,2880]{1,0:T(8,128)S(1)}) fusion(bf16[128,2880]{0,1:T(8,128)(2,1)} %param.9, s32[128]{0:T(128)S(1)} %add_reduce_fusion, pred[128]{0:T(512)(128)(4,1)S(1)} %broadcast_compare_fusion), kind=kOutput, calls=%fused_computation.24 | convolution fusion | flops 17839080 | bytes 1014496 | tf_op jit(solution)/shard_map/dot_general | solution.py:26
  11.1 1.3 dynamic-slice
  12.4 0.8 multiply_convert_fusion
  13.2 1.4 %dynamic-update-slice = s32[4]{0:T(128)S(1)} dynamic-update-slice(s32[4]{0:T(128)S(1)} %broadcast.62, s32[1]{0:T(128)} %bitcast.1, u32[]{:T(128)} %bitcast.2) | dynamic-update-slice | bytes 12
  14.7 17.8 %all_gather.7 = bf16[96,2880]{1,0:T(8,128)(2,1)S(1)} all-gather(bf16[24,2880]{1,0:T(8,128)(2,1)S(1)} %multiply_convert_fusion), channel_id=1, replica_groups=mesh['dp'=4,'expert'=8] {'dp'}, dimensions={0}, use_global_device_ids=true | all-gather | bytes 691200 | tf_op jit(solution)/shard_map/all_gather | solution.py:30
  32.5 8.4 %all-reduce = s32[4]{0:T(128)S(1)} all-reduce(s32[4]{0:T(128)S(1)} %dynamic-update-slice), channel_id=1, replica_groups=mesh['dp'=4,'expert'=8] {'dp'}, use_global_device_ids=true, to_apply=%add | all-reduce | flops 4 | bytes 32
  41.0 0.2 reduce-window.18
  41.3 0.8 copy.47
  42.3 0.2 reduce_window_sum.25
  42.5 0.2 select_reduce_fusion.1
  42.8 0.7 add_bitcast_fusion
  43.7 0.5 convolution_convert_fusion
  44.2 0.2 all_to_all.30
  44.5 19.8 %all_to_all.43 = bf16[8,20,2880]{2,1,0:T(8,128)(2,1)S(1)} all-to-all(bf16[8,20,2880]{2,1,0:T(8,128)(2,1)S(1)} %all_to_all.30), channel_id=1, replica_groups=mesh['dp'=4,'expert'=8] {'expert'}, dimensions={0} | all-to-all | bytes 1843200 | tf_op jit(solution)/shard_map/all_to_all | solution.py:50
  64.3 0.4 all_to_all.32
  64.7 3.7 %fusion.2 = f32[160,720]{1,0:T(8,128)S(1)} fusion(bf16[160,2880]{1,0:T(8,128)(2,1)S(1)} %all_to_all.32, bf16[1,2880,720]{1,2,0:T(8,128)(2,1)} %param.15), kind=kOutput, calls=%fused_computation.2 | convolution fusion | flops 663552000 | bytes 5529600 | tf_op jit(solution)/shard_map/dot_general | solution.py:51
  68.3 6.4 %fusion.7 = bf16[160,2880]{1,0:T(8,128)(2,1)S(1)} fusion(bf16[1,720,2880]{2,1,0:T(8,128)(2,1)} %param.17, f32[160,720]{1,0:T(8,128)S(1)} %fusion.2, bf16[160,2880]{1,0:T(8,128)(2,1)S(1)} %all_to_all.32, bf16[1,2880,720]{1,2,0:T(8,128)(2,1)} %param.16), kind=kOutput, calls=%fused_computation.8 | convolution fusion | flops 1328486400 | bytes 10598400 | tf_op jit(solution)/shard_map/dot_general | solution.py:54
  74.8 1.7 %copy.51 = bf16[160,2880]{0,1:T(8,128)(2,1)} copy(bf16[160,2880]{1,0:T(8,128)(2,1)S(1)} %fusion.7) | data formatting | bytes 1843200
  76.7 31.5 %reduce-scatter.4.cloned.1.call-done = bf16[720,160]{1,0:T(8,128)(2,1)} async-done(((bf16[2880,160]{1,0:T(8,128)(2,1)}), bf16[720,160]{1,0:T(8,128)(2,1)}) %reduce-scatter.4.cloned.1.call-update) | async-done | bytes 230416
  108.3 1.1 copy.52
  109.4 0.8 all_to_all.33
  110.2 3.7 %all-to-all-start.1 = ((bf16[8,20,720]{2,1,0:T(8,128)(2,1)}), bf16[8,20,720]{2,1,0:T(8,128)(2,1)S(1)}, u32[]{:S(2)}, u32[]{:S(2)}) async-start(bf16[8,20,720]{2,1,0:T(8,128)(2,1)} %all_to_all.33), calls=%async_computation.1 | async-start | bytes 589824 | tf_op jit(solution)/shard_map/all_to_all | solution.py:56
  113.9 7.2 %all-to-all-done.1 = bf16[8,20,720]{2,1,0:T(8,128)(2,1)S(1)} async-done(((bf16[8,20,720]{2,1,0:T(8,128)(2,1)}), bf16[8,20,720]{2,1,0:T(8,128)(2,1)S(1)}, u32[]{:S(2)}, u32[]{:S(2)}) %all-to-all-start.1) | async-done | bytes 230432 | tf_op jit(solution)/shard_map/all_to_all | solution.py:56
  121.2 0.2 convolution_convert_fusion.3
  121.4 0.2 convolution_convert_fusion.2
  121.7 9.1 %all_to_all.44 = bf16[4,24,720]{2,1,0:T(8,128)(2,1)S(1)} all-to-all(bf16[4,24,720]{2,1,0:T(8,128)(2,1)S(1)} %bitcast.46), channel_id=1, replica_groups=mesh['dp'=4,'expert'=8] {'dp'}, dimensions={0} | all-to-all | bytes 276480 | tf_op jit(solution)/shard_map/all_to_all | solution.py:67
  130.8 0.2 all_to_all.39
  131.0 1.3 fusion.10
  (29 shorter events, 1.4 us)
Async XLA Ops:
  6.5 101.7 %reduce-scatter.4.cloned.1.call-start = ((), (), s32[]{:S(2)}) async-start(), calls=%async_computation.4 | async-start | bytes 1843200
  74.8 39.0 %copy-start.1 = (s32[1,32,4]{1,2,0:T(4,128)S(1)}, s32[1,32,4]{1,2,0:T(4,128)}, u32[]{:S(2)}) copy-start(s32[1,32,4]{1,2,0:T(4,128)} %param.13) | copy-start | bytes 1540
  74.8 39.0 %copy-start.2 = (f32[1,32,4]{1,2,0:T(4,128)S(1)}, f32[1,32,4]{1,2,0:T(4,128)}, u32[]{:S(2)}) copy-start(f32[1,32,4]{1,2,0:T(4,128)} %param.14) | copy-start | bytes 1540
  74.8 56.1 %copy-start = (bf16[128,2880]{0,1:T(8,128)(2,1)S(1)}, bf16[128,2880]{0,1:T(8,128)(2,1)}, u32[]{:S(2)}) copy-start(bf16[128,2880]{0,1:T(8,128)(2,1)} %param.9) | copy-start | bytes 2211844
  74.8 56.1 %copy-start.3 = (f32[128]{0:T(128)S(1)}, f32[128]{0:T(128)}, u32[]{:S(2)}) copy-start(f32[128]{0:T(128)} %param.11) | copy-start | bytes 1540
  110.2 10.9 %all-to-all-start.1 = ((bf16[8,20,720]{2,1,0:T(8,128)(2,1)}), bf16[8,20,720]{2,1,0:T(8,128)(2,1)S(1)}, u32[]{:S(2)}, u32[]{:S(2)}) async-start(bf16[8,20,720]{2,1,0:T(8,128)(2,1)} %all_to_all.33), calls=%async_computation.1 | async-start | bytes 589824 | tf_op jit(solution)/shard_map/all_to_all | solution.py:56
Sparse Core Ops, SparseCore 0:
  76.7 31.5 reduce-scatter.3
where the time goes:
time: 140 us; the launch traced here: 139 us
  blocking collectives  55 us (39%)
  waiting for transfers between devices  38.7 us (28%)
  matrix products  13.9 us (10%)
  between operations  13.6 us (10%)
  local copies, waits for them, and re-layouts  9.46 us (7%)
  other arithmetic  4.69 us (3%)
  starting transfers between devices  3.66 us (3%)
    unnamed x2, waiting for transfers between devices  31.6 us
    all_to_all x1, blocking collectives, local(): lax.all_to_all(buffer, 'expert', split_axis=0, concat_axis=0, tiled=True)  19.8 us
    all_gather x1, blocking collectives, local(): lax.all_gather(normalized_rows, 'dp', axis=0, tiled=True)  17.8 us
    all_to_all x1, blocking collectives, local(): lax.all_to_all(owned, 'dp', split_axis=0, concat_axis=1, tiled=True)  9.05 us
    unnamed x1, blocking collectives  8.39 us
    all_to_all x1, waiting for transfers between devices, local(): lax.all_to_all(summed, 'expert', split_axis=0, concat_axis=0, tiled=True)  7.15 us
    dot_general x1, matrix products, local(): partials = jnp.dot(hidden, w_down[0], preferred_element_type=jnp.float32)  6.44 us
    unnamed x14, local copies, waits for them, and re-layouts  6.36 us
  transfers between devices with their start and end apart: 2, of which 2 were waited for; matrix products, arithmetic and copies ran while one was open for 0% of the time, Pallas kernels for 0%

commit v1 on v0

--- a/solution.py
+++ b/solution.py
@@ -1,7 +1,313 @@
 import jax
 import jax.numpy as jnp
 from jax import lax
+from jax.experimental import pallas as pl
+from jax.experimental.pallas import tpu as pltpu
 from jax.sharding import PartitionSpec as P
+
+CHUNK = 768
+LANES = 128
+HALF = 16
+
+
+def chunks_of(width):
+    starts = list(range(0, width, CHUNK))
+    return [(s, min(CHUNK, width - s)) for s in starts]
+
+
+def fused_kernel(
+    tokens_hbm, passes_ref, keep_ref, gain_ref, routes_ref, gates_ref, wg_hbm, wu_hbm, wd_hbm,
+    out_ref,
+    tokens, wg, wu, wd, cnt, gb, own, zin, zsend, tot, x, acc_g, acc_u, hid, ob, rb, sb, rr,
+    ret, zin2, zsend2,
+    ld_sem, cnt_s, cnt_r, gb_s, gb_r, z_s, z_r, a_s, a_r, b_s, b_r, d_s, d_r, e_s, e_r, z2_s, z2_r,
+):
+    z, me = lax.axis_index("dp"), lax.axis_index("expert")
+    n_z, n_e = lax.axis_size("dp"), lax.axis_size("expert")
+    width = tokens.shape[1]
+    chunks = chunks_of(width)
+    n_c = len(chunks)
+    span = [pl.ds(0, -(-w // LANES) * LANES) for _, w in chunks]
+    core = lax.rem(me, 2)
+    sibling = me + 1 - 2 * core
+    low = z < 2
+    edge = jnp.logical_or(z == 0, z == n_z - 1)
+    middle = jnp.logical_not(edge)
+    inward = jnp.where(low, z + 1, z - 1)
+    outward = jnp.where(z == 1, 0, n_z - 1)
+    lands = jnp.where(edge, 0, 1)
+    f32, bf16 = jnp.float32, jnp.bfloat16
+
+    loads = [
+        pltpu.make_async_copy(tokens_hbm, tokens, ld_sem.at[0]),
+        pltpu.make_async_copy(wg_hbm, wg, ld_sem.at[1]),
+        pltpu.make_async_copy(wu_hbm, wu, ld_sem.at[2]),
+        pltpu.make_async_copy(wd_hbm, wd, ld_sem.at[3]),
+    ]
+    for load in loads:
+        load.start()
+
+    barrier = pltpu.get_barrier_semaphore()
+    for r in range(1, n_z):
+        pl.semaphore_signal(barrier, inc=1, device_id={"dp": lax.rem(z + r, n_z)})
+    for r in range(1, n_e):
+        pl.semaphore_signal(barrier, inc=1, device_id={"expert": lax.rem(me + r, n_e)})
+
+    flags = passes_ref[...].astype(f32)
+    t_tok = flags.shape[1]
+    sub = lax.broadcasted_iota(jnp.int32, (t_tok, t_tok), 0)
+    lane = lax.broadcasted_iota(jnp.int32, (t_tok, t_tok), 1)
+    wide = jnp.broadcast_to(flags, (t_tok, t_tok))
+    rank_col = jnp.sum(jnp.where(lane <= sub, wide, 0.0), axis=1, keepdims=True) - 1.0
+    flag_col = jnp.sum(jnp.where(lane == sub, wide, 0.0), axis=1, keepdims=True)
+    keep_col = jnp.sum(
+        jnp.where(lane == sub, jnp.broadcast_to(keep_ref[...], (t_tok, t_tok)), 0.0),
+        axis=1, keepdims=True,
+    )
+    rank_row = jnp.sum(jnp.where(sub <= lane, flag_col, 0.0), axis=0, keepdims=True) - 1.0
+
+    cnt[z] = jnp.broadcast_to(flags, cnt.shape[1:])
+    seq_keep, top = routes_ref.shape
+    e_lane = lax.broadcasted_iota(jnp.int32, (seq_keep, LANES), 1)
+    weights = jnp.zeros((seq_keep, LANES), f32)
+    for k in range(top):
+        weights += jnp.where(routes_ref[:, k:k + 1] == e_lane, gates_ref[:, k:k + 1], 0.0)
+    gb[:, me] = weights.reshape(2, HALF, LANES)
+
+    pl.semaphore_wait(barrier, n_z - 1 + n_e - 1)
+    sends = []
+
+    def send(src, dst, ssem, rsem, device):
+        copy = pltpu.make_async_remote_copy(
+            src_ref=src, dst_ref=dst, send_sem=ssem, recv_sem=rsem, device_id=device,
+            device_id_type=pl.DeviceIdType.MESH,
+        )
+        copy.start()
+        return copy
+
+    def arrived(ref, sem):
+        pltpu.make_async_copy(ref, ref, sem).wait()
+
+    for r in range(1, n_z):
+        sends.append(send(cnt.at[z], cnt.at[z], cnt_s.at[r - 1], cnt_r, {"dp": lax.rem(z + r, n_z)}))
+    for r in range(1, n_e):
+        sends.append(
+            send(gb.at[:, me], gb.at[:, me], gb_s.at[r - 1], gb_r, {"expert": lax.rem(me + r, n_e)})
+        )
+
+    loads[0].wait()
+    arrived(cnt.at[pl.ds(0, n_z - 1)], cnt_r)
+    offset = jnp.zeros((1, 1), f32)
+    for other in range(n_z):
+        total = jnp.sum(cnt[other, 0:1, :], axis=1, keepdims=True)
+        offset += jnp.where(other < z, total, 0.0)
+    s_sub = lax.broadcasted_iota(jnp.int32, (seq_keep, t_tok), 0).astype(f32)
+    picker = jnp.where((rank_row + offset == s_sub) & (flags > 0.5), 1.0, 0.0).astype(bf16)
+    s_lane = lax.broadcasted_iota(jnp.int32, (t_tok, seq_keep), 1).astype(f32)
+    spread_pick = jnp.where((rank_col + offset == s_lane) & (flag_col > 0.5), 1.0, 0.0).astype(bf16)
+
+    compact = jnp.dot(picker, tokens[...], preferred_element_type=f32)
+    scaling = lax.rsqrt(jnp.sum(compact * compact, axis=1, keepdims=True) * (1.0 / width) + 1e-05)
+    normed = (compact * scaling * gain_ref[...]).astype(bf16)
+
+    @pl.when(edge)
+    def _():
+        zin[0] = jnp.zeros_like(zin[0])
+        zin2[0] = jnp.zeros_like(zin2[0])
+
+    for k, (start, w) in enumerate(chunks):
+        own[k, :, 0:w] = normed[:, start:start + w]
+
+    def line_copy(src, dst, k, which, s_sems, r_sems, device):
+        return pltpu.make_async_remote_copy(
+            src_ref=src, dst_ref=dst, send_sem=s_sems.at[which, k], recv_sem=r_sems,
+            device_id={"dp": device}, device_id_type=pl.DeviceIdType.MESH,
+        )
+
+    def near(k, mine, into, out, s_sems, r_sems):
+        @pl.when(middle)
+        def _():
+            arrived(into.at[0, k, :, span[k]], r_sems.at[0, k])
+
+        out[0, k] = (mine[k].astype(f32) + into[0, k].astype(f32)).astype(bf16)
+        line_copy(
+            out.at[0, k, :, span[k]], into.at[lands, k, :, span[k]], k, 0, s_sems,
+            r_sems.at[lands, k], inward,
+        ).start()
+
+    def far(k, mine, into, out, s_sems, r_sems):
+        arrived(into.at[1, k, :, span[k]], r_sems.at[1, k])
+        part = mine[k].astype(f32) + into[1, k].astype(f32)
+
+        @pl.when(middle)
+        def _():
+            out[1, k] = part.astype(bf16)
+            line_copy(
+                out.at[1, k, :, span[k]], into.at[1, k, :, span[k]], k, 1, s_sems,
+                r_sems.at[1, k], outward,
+            ).start()
+
+        return (part + into[0, k].astype(f32)).astype(bf16)
+
+    def line_drain(k, out, s_sems):
+        arrived(out.at[0, k, :, span[k]], s_sems.at[0, k])
+
+        @pl.when(middle)
+        def _():
+            arrived(out.at[1, k, :, span[k]], s_sems.at[1, k])
+
+    line_in = (own, zin, zsend, z_s, z_r)
+    line_out = (ret, zin2, zsend2, z2_s, z2_r)
+
+    def s_near(k):
+        near(k, *line_in)
+
+    def s_far(k):
+        tot[k] = far(k, *line_in).reshape(2, HALF, CHUNK)
+        x[k, core, me] = tot[k, core]
+        for r in range(1, n_e):
+            to = lax.rem(me + r, n_e)
+            side = lax.rem(to, 2)
+            sends.append(send(
+                tot.at[k, side, :, span[k]], x.at[k, side, me, :, span[k]],
+                a_s.at[k, r - 1], a_r.at[k], {"expert": to},
+            ))
+
+    def s_swap(k):
+        arrived(x.at[k, core, pl.ds(0, n_e - 1), :, span[k]], a_r.at[k])
+        block = x.at[k, core, :, :, span[k]]
+        sends.append(send(block, block, b_s.at[k], b_r.at[k], {"expert": sibling}))
+
+    def s_up(k):
+        start, w = chunks[k]
+        arrived(x.at[k, 1 - core, :, :, span[k]], b_r.at[k])
+        if k == 0:
+            loads[1].wait()
+            loads[2].wait()
+        rows = x[k].reshape(2 * n_e * HALF, CHUNK)[:, 0:w]
+        g = jnp.dot(rows, wg[start:start + w, :], preferred_element_type=f32)
+        u = jnp.dot(rows, wu[start:start + w, :], preferred_element_type=f32)
+        if k == 0:
+            acc_g[...] = g
+            acc_u[...] = u
+        else:
+            acc_g[...] += g
+            acc_u[...] += u
+
+    def skewed(stages):
+        for t in range(n_c + len(stages) - 1):
+            for i, stage in enumerate(stages):
+                if 0 <= t - i < n_c:
+                    stage(t - i)
+
+    skewed([s_near, s_far, s_swap, s_up])
+
+    arrived(gb.at[:, pl.ds(0, n_e - 1)], gb_r)
+    g_lane = lax.broadcasted_iota(jnp.int32, gb.shape, 3)
+    gw = jnp.sum(jnp.where(g_lane == me, gb[...], 0.0), axis=3, keepdims=True)
+    gw = gw.reshape(2 * n_e * HALF, 1)
+    gate = acc_g[...]
+    hid[...] = ((acc_u[...] + 1.0) * gate * jax.nn.sigmoid(1.702 * gate) * gw).astype(bf16)
+    loads[3].wait()
+
+    def s_down(k):
+        start, w = chunks[k]
+        part = jnp.dot(hid[...], wd[:, start:start + w], preferred_element_type=f32).astype(bf16)
+        ob[k, :, :, :, 0:w] = part.reshape(2, n_e, HALF, w)
+        sends.append(send(
+            ob.at[k, 1 - core, :, :, span[k]], rb.at[k, :, :, span[k]],
+            d_s.at[k], d_r.at[k], {"expert": sibling},
+        ))
+
+    def s_pair(k):
+        arrived(rb.at[k, :, :, span[k]], d_r.at[k])
+        sb[k] = (ob[k, core].astype(f32) + rb[k].astype(f32)).astype(bf16)
+        rr[k, me] = sb[k, me]
+        for r in range(1, n_e):
+            to = lax.rem(me + r, n_e)
+            sends.append(send(
+                sb.at[k, to, :, span[k]], rr.at[k, me, :, span[k]],
+                e_s.at[k, r - 1], e_r.at[k], {"expert": to},
+            ))
+
+    def s_sum(k):
+        arrived(rr.at[k, pl.ds(0, n_e - 1), :, span[k]], e_r.at[k])
+        halves = [
+            sum(rr[k, 2 * j + h].astype(f32) for j in range(n_e // 2)) for h in range(2)
+        ]
+        ret[k, 0:HALF] = halves[0].astype(bf16)
+        ret[k, HALF:2 * HALF] = halves[1].astype(bf16)
+
+    def s_near2(k):
+        near(k, *line_out)
+
+    def s_far2(k):
+        start, w = chunks[k]
+        mixture = far(k, *line_out)[:, 0:w]
+        spread = jnp.dot(spread_pick, mixture, preferred_element_type=f32)
+        out_ref[:, start:start + w] = (
+            tokens[:, start:start + w].astype(f32) + keep_col * spread
+        ).astype(bf16)
+
+    skewed([s_down, s_pair, s_sum, s_near2, s_far2])
+
+    for copy in sends:
+        copy.wait_send()
+    for k in range(n_c):
+        line_drain(k, zsend, z_s)
+        line_drain(k, zsend2, z2_s)
+
+
+def fused(tokens, passes, keep, gain, routes, gates, wg, wu, wd):
+    n_z, n_e = lax.axis_size("dp"), lax.axis_size("expert")
+    t_tok, width = tokens.shape
+    seq_keep = routes.shape[1]
+    hidden = wg.shape[2]
+    n_c = len(chunks_of(width))
+    bf16, f32 = jnp.bfloat16, jnp.float32
+    vmem = pl.BlockSpec(memory_space=pltpu.VMEM)
+    hbm = pl.BlockSpec(memory_space=pl.ANY)
+    dma = pltpu.SemaphoreType.DMA
+    rows = n_e * seq_keep
+    line = pltpu.VMEM((2, n_c, seq_keep, CHUNK), bf16)
+    single = pltpu.VMEM((n_c, seq_keep, CHUNK), bf16)
+    block = pltpu.VMEM((n_c, n_e, HALF, CHUNK), bf16)
+    both = pltpu.VMEM((n_c, 2, n_e, HALF, CHUNK), bf16)
+    return pl.pallas_call(
+        fused_kernel,
+        out_shape=jax.ShapeDtypeStruct((t_tok, width), bf16),
+        in_specs=[hbm, vmem, vmem, vmem, vmem, vmem, hbm, hbm, hbm],
+        out_specs=vmem,
+        scratch_shapes=[
+            pltpu.VMEM((t_tok, width), bf16),
+            pltpu.VMEM(wg.shape[1:], bf16),
+            pltpu.VMEM(wu.shape[1:], bf16),
+            pltpu.VMEM(wd.shape[1:], bf16),
+            pltpu.VMEM((n_z, 8, t_tok), f32),
+            pltpu.VMEM((2, n_e, HALF, LANES), f32),
+            single, line, line,
+            pltpu.VMEM((n_c, 2, HALF, CHUNK), bf16),
+            both,
+            pltpu.VMEM((rows, hidden), f32),
+            pltpu.VMEM((rows, hidden), f32),
+            pltpu.VMEM((rows, hidden), bf16),
+            both, block, block, block,
+            single, line, line,
+            dma((4,)), dma((n_z - 1,)), dma, dma((n_e - 1,)), dma,
+            dma((2, n_c)), dma((2, n_c)),
+            dma((n_c, n_e - 1)), dma((n_c,)),
+            dma((n_c,)), dma((n_c,)),
+            dma((n_c,)), dma((n_c,)),
+            dma((n_c, n_e - 1)), dma((n_c,)),
+            dma((2, n_c)), dma((2, n_c)),
+        ],
+        compiler_params=pltpu.CompilerParams(
+            collective_id=0, has_side_effects=True, vmem_limit_bytes=48 * 1024 * 1024
+        ),
+    )(
+        tokens, passes.reshape(1, t_tok), keep.reshape(1, t_tok), gain.reshape(1, width),
+        routes[0], gates[0], wg[0], wu[0], wd[0],
+    )
 
 
 def rescaled_entries(rows_in, gain_row):
@@ -70,9 +376,18 @@
     return result.astype(jnp.bfloat16)
 
 
+def layer(tokens, passes_through, keep_weight, norm_gain, routes, gate_values, w_gate, w_up, w_down):
+    lines, experts = lax.axis_size("dp"), lax.axis_size("expert")
+    fits = lines == 4 and experts % 2 == 0 and experts * routes.shape[1] <= 512
+    step = fused if fits and routes.shape[1] == 2 * HALF and experts <= LANES else local
+    return step(
+        tokens, passes_through, keep_weight, norm_gain, routes, gate_values, w_gate, w_up, w_down
+    )
+
+
 def solution(mesh):
     return jax.shard_map(
-        local,
+        layer,
         mesh=mesh,
         in_specs=(
             P(("expert", "dp"), None),

time: 140 us -> 96.3 us (0.69)
  Pallas kernels: 0 us -> 75.6 us
  blocking collectives: 55 us -> 0 us
  waiting for transfers between devices: 38.7 us -> 0 us
  matrix products: 13.9 us -> 0 us
  between operations: 13.6 us -> 0.02 us
  local copies, waits for them, and re-layouts: 9.46 us -> 20.1 us
  other arithmetic: 4.69 us -> 0 us
  starting transfers between devices: 3.66 us -> 0 us
    pallas_call x0 -> x1, Pallas kernels: none -> 75.6 us  [fused(): pl.pallas_call(fused_kernel, out_shape=jax.ShapeDtypeStruct((t_tok, width...]
    unnamed x2 -> x0, waiting for transfers between devices: 31.6 us -> none
    all_to_all x2 -> x0, blocking collectives: 28.8 us -> none  [the longest x1 19.8 us: local(): lax.all_to_all(buffer, 'expert', split_axis=0, concat_axis=0, tiled=True)]
    all_gather x1 -> x0, blocking collectives: 17.8 us -> none  [local(): lax.all_gather(normalized_rows, 'dp', axis=0, tiled=True)]
    dot_general x7 -> x0, matrix products: 13.9 us -> none  [the longest x1 6.44 us: local(): partials = jnp.dot(hidden, w_down[0], preferred_element_type=jnp.float32)]
    unnamed x14 -> x9, local copies, waits for them, and re-layouts: 6.36 us -> 16.7 us
    unnamed x1 -> x0, blocking collectives: 8.39 us -> none
    all_to_all x1 -> x0, waiting for transfers between devices: 7.15 us -> none  [local(): lax.all_to_all(summed, 'expert', split_axis=0, concat_axis=0, tiled=True)]
  transfers between devices with their start and end apart: 2 -> 0, of which waited for: 2 -> 0; matrix products, arithmetic and copies ran while one was open for 0% -> 0% of each run, Pallas kernels for 0% -> 0%
where the time goes in v1:
time: 96.3 us; the launch traced here: 95.8 us
  Pallas kernels  75.6 us (79%)
  local copies, waits for them, and re-layouts  20.1 us (21%)
    pallas_call x1, Pallas kernels, fused(): pl.pallas_call(fused_kernel, out_shape=jax.ShapeDtypeStruct((t_tok, width...  75.6 us
    unnamed x9, local copies, waits for them, and re-layouts  16.7 us

profile of v1, /device:TPU:0, one launch (start us, length us, event | category | flops | bytes accessed | tf_op | source)
XLA Modules:
  0.0 95.8 jit_solution(9134518950385061092)
XLA Ops:
  0.0 0.7 reshape.11.gain_ref
  0.7 0.8 copy.13.routes_ref
  1.5 0.8 copy.14.gates_ref
  2.2 1.5 %copy.12.tokens_hbm = bf16[128,2880]{1,0:T(8,128)(2,1)S(1)} copy(bf16[128,2880]{0,1:T(8,128)(2,1)} %param.9) | data formatting | bytes 1474560 | tf_op args[0]
  3.7 6.5 %copy.10 = bf16[1,2880,720]{2,1,0:T(8,128)(2,1)} copy(bf16[1,2880,720]{1,2,0:T(8,128)(2,1)} %param.15) | data formatting | bytes 8294400 | tf_op args[6]
  10.2 0.0 copy-start.1
  10.2 0.0 copy-start.2
  10.2 6.5 %copy.11 = bf16[1,2880,720]{2,1,0:T(8,128)(2,1)} copy(bf16[1,2880,720]{1,2,0:T(8,128)(2,1)} %param.16) | data formatting | bytes 8294400 | tf_op args[7]
  16.8 0.0 copy-done.1
  16.8 0.0 copy-done.2
  16.8 0.0 copy-start
  16.8 2.2 %copy-done = bf16[1,720,2880]{2,1,0:T(8,128)(2,1)S(1)} copy-done((bf16[1,720,2880]{2,1,0:T(8,128)(2,1)S(1)}, bf16[1,720,2880]{2,1,0:T(8,128)(2,1)}, u32[]{:S(2)}) %copy-start) | copy-done | bytes 4147224
  19.0 75.6 %shard_map.91 = bf16[128,2880]{1,0:T(8,128)(2,1)S(1)} custom-call(bf16[128,2880]{1,0:T(8,128)(2,1)S(1)} %copy.12.tokens_hbm, s32[1,128]{1,0:T(1,128)S(1)} %bitcast.8, f32[1,128]{1,0:T(1,128)S(1)} %bitcast.9, f32[1,2880]{1,0:T(1,128)S(1)} %reshape.11.gain_ref, s32[32,4]{1,0:T(8,128)S(1)} %copy.13.routes_ref, f32[32,4]{1,0:T(8,128)S(1)} %copy.14.gates_ref, ...), custom_call_target="tpu_custom_call" | custom-call | tf_op jit(solution)/shard_map/pallas_call | solution.py:276
  94.6 1.2 %copy.15 = bf16[128,2880]{0,1:T(8,128)(2,1)} copy(bf16[128,2880]{1,0:T(8,128)(2,1)S(1)} %shard_map.91) | data formatting | bytes 1474560 | tf_op jit(solution)/shard_map/pallas_call | solution.py:276
Async XLA Ops:
  10.2 6.5 %copy-start.1 = (s32[128]{0:T(128)S(1)}, s32[128]{0:T(128)}, u32[]{:S(2)}) copy-start(s32[128]{0:T(128)} %param.10) | copy-start | bytes 1540
  10.2 6.5 %copy-start.2 = (f32[128]{0:T(128)S(1)}, f32[128]{0:T(128)}, u32[]{:S(2)}) copy-start(f32[128]{0:T(128)} %param.11) | copy-start | bytes 1540
  16.8 2.2 %copy-start = (bf16[1,720,2880]{2,1,0:T(8,128)(2,1)S(1)}, bf16[1,720,2880]{2,1,0:T(8,128)(2,1)}, u32[]{:S(2)}) copy-start(bf16[1,720,2880]{2,1,0:T(8,128)(2,1)} %param.17) | copy-start | bytes 12441604

commit v2 on v1

--- a/solution.py
+++ b/solution.py
@@ -5,9 +5,11 @@
 from jax.experimental.pallas import tpu as pltpu
 from jax.sharding import PartitionSpec as P
 
-CHUNK = 768
+CHUNK = 1536
 LANES = 128
 HALF = 16
+NT = (((1,), (1,)), ((), ()))
+TN = (((0,), (0,)), ((), ()))
 
 
 def chunks_of(width):
@@ -24,7 +26,7 @@
 ):
     z, me = lax.axis_index("dp"), lax.axis_index("expert")
     n_z, n_e = lax.axis_size("dp"), lax.axis_size("expert")
-    width = tokens.shape[1]
+    width = tokens.shape[0]
     chunks = chunks_of(width)
     n_c = len(chunks)
     span = [pl.ds(0, -(-w // LANES) * LANES) for _, w in chunks]
@@ -58,20 +60,26 @@
     sub = lax.broadcasted_iota(jnp.int32, (t_tok, t_tok), 0)
     lane = lax.broadcasted_iota(jnp.int32, (t_tok, t_tok), 1)
     wide = jnp.broadcast_to(flags, (t_tok, t_tok))
-    rank_col = jnp.sum(jnp.where(lane <= sub, wide, 0.0), axis=1, keepdims=True) - 1.0
     flag_col = jnp.sum(jnp.where(lane == sub, wide, 0.0), axis=1, keepdims=True)
-    keep_col = jnp.sum(
-        jnp.where(lane == sub, jnp.broadcast_to(keep_ref[...], (t_tok, t_tok)), 0.0),
-        axis=1, keepdims=True,
-    )
     rank_row = jnp.sum(jnp.where(sub <= lane, flag_col, 0.0), axis=0, keepdims=True) - 1.0
 
     cnt[z] = jnp.broadcast_to(flags, cnt.shape[1:])
-    seq_keep, top = routes_ref.shape
+    top, seq_keep = routes_ref.shape
+    diagonal = lax.broadcasted_iota(jnp.int32, (seq_keep, seq_keep), 0) == (
+        lax.broadcasted_iota(jnp.int32, (seq_keep, seq_keep), 1)
+    )
+
+    def as_column(row):
+        square = jnp.broadcast_to(row, (seq_keep, seq_keep))
+        return jnp.sum(jnp.where(diagonal, square, jnp.zeros_like(square)), axis=1, keepdims=True)
+
     e_lane = lax.broadcasted_iota(jnp.int32, (seq_keep, LANES), 1)
     weights = jnp.zeros((seq_keep, LANES), f32)
     for k in range(top):
-        weights += jnp.where(routes_ref[:, k:k + 1] == e_lane, gates_ref[:, k:k + 1], 0.0)
+        weights += jnp.where(
+            as_column(routes_ref[k:k + 1, :].astype(f32)) == e_lane.astype(f32),
+            as_column(gates_ref[k:k + 1, :]), 0.0,
+        )
     gb[:, me] = weights.reshape(2, HALF, LANES)
 
     pl.semaphore_wait(barrier, n_z - 1 + n_e - 1)
@@ -103,10 +111,7 @@
         offset += jnp.where(other < z, total, 0.0)
     s_sub = lax.broadcasted_iota(jnp.int32, (seq_keep, t_tok), 0).astype(f32)
     picker = jnp.where((rank_row + offset == s_sub) & (flags > 0.5), 1.0, 0.0).astype(bf16)
-    s_lane = lax.broadcasted_iota(jnp.int32, (t_tok, seq_keep), 1).astype(f32)
-    spread_pick = jnp.where((rank_col + offset == s_lane) & (flag_col > 0.5), 1.0, 0.0).astype(bf16)
-
-    compact = jnp.dot(picker, tokens[...], preferred_element_type=f32)
+    compact = lax.dot_general(picker, tokens[...], NT, preferred_element_type=f32)
     scaling = lax.rsqrt(jnp.sum(compact * compact, axis=1, keepdims=True) * (1.0 / width) + 1e-05)
     normed = (compact * scaling * gain_ref[...]).astype(bf16)
 
@@ -185,8 +190,8 @@
             loads[1].wait()
             loads[2].wait()
         rows = x[k].reshape(2 * n_e * HALF, CHUNK)[:, 0:w]
-        g = jnp.dot(rows, wg[start:start + w, :], preferred_element_type=f32)
-        u = jnp.dot(rows, wu[start:start + w, :], preferred_element_type=f32)
+        g = lax.dot_general(rows, wg[:, start:start + w], NT, preferred_element_type=f32)
+        u = lax.dot_general(rows, wu[:, start:start + w], NT, preferred_element_type=f32)
         if k == 0:
             acc_g[...] = g
             acc_u[...] = u
@@ -244,9 +249,9 @@
     def s_far2(k):
         start, w = chunks[k]
         mixture = far(k, *line_out)[:, 0:w]
-        spread = jnp.dot(spread_pick, mixture, preferred_element_type=f32)
-        out_ref[:, start:start + w] = (
-            tokens[:, start:start + w].astype(f32) + keep_col * spread
+        spread = lax.dot_general(mixture, picker, TN, preferred_element_type=f32)
+        out_ref[start:start + w, :] = (
+            tokens[start:start + w, :].astype(f32) + keep_ref[...] * spread
         ).astype(bf16)
 
     skewed([s_down, s_pair, s_sum, s_near2, s_far2])
@@ -263,6 +268,7 @@
     t_tok, width = tokens.shape
     seq_keep = routes.shape[1]
     hidden = wg.shape[2]
+    turned = lambda w: jnp.swapaxes(w[0], 0, 1)
     n_c = len(chunks_of(width))
     bf16, f32 = jnp.bfloat16, jnp.float32
     vmem = pl.BlockSpec(memory_space=pltpu.VMEM)
@@ -275,13 +281,13 @@
     both = pltpu.VMEM((n_c, 2, n_e, HALF, CHUNK), bf16)
     return pl.pallas_call(
         fused_kernel,
-        out_shape=jax.ShapeDtypeStruct((t_tok, width), bf16),
+        out_shape=jax.ShapeDtypeStruct((width, t_tok), bf16),
         in_specs=[hbm, vmem, vmem, vmem, vmem, vmem, hbm, hbm, hbm],
         out_specs=vmem,
         scratch_shapes=[
-            pltpu.VMEM((t_tok, width), bf16),
-            pltpu.VMEM(wg.shape[1:], bf16),
-            pltpu.VMEM(wu.shape[1:], bf16),
+            pltpu.VMEM((width, t_tok), bf16),
+            pltpu.VMEM((hidden, width), bf16),
+            pltpu.VMEM((hidden, width), bf16),
             pltpu.VMEM(wd.shape[1:], bf16),
             pltpu.VMEM((n_z, 8, t_tok), f32),
             pltpu.VMEM((2, n_e, HALF, LANES), f32),
@@ -302,12 +308,12 @@
             dma((2, n_c)), dma((2, n_c)),
         ],
         compiler_params=pltpu.CompilerParams(
-            collective_id=0, has_side_effects=True, vmem_limit_bytes=48 * 1024 * 1024
+            collective_id=0, has_side_effects=True, vmem_limit_bytes=58 * 1024 * 1024
         ),
     )(
-        tokens, passes.reshape(1, t_tok), keep.reshape(1, t_tok), gain.reshape(1, width),
-        routes[0], gates[0], wg[0], wu[0], wd[0],
-    )
+        tokens.T, passes.reshape(1, t_tok), keep.reshape(1, t_tok), gain.reshape(1, width),
+        turned(routes), turned(gates), turned(wg), turned(wu), wd[0],
+    ).T
 
 
 def rescaled_entries(rows_in, gain_row):

time: 96.3 us -> 63 us (0.65)
  local copies, waits for them, and re-layouts: 20.1 us -> 3.34 us
  Pallas kernels: 75.6 us -> 59.4 us
    pallas_call x1, Pallas kernels: 75.6 us -> 59.4 us  [fused(): pl.pallas_call(fused_kernel, out_shape=jax.ShapeDtypeStruct((width, t_tok...]
    unnamed x9 -> x1, local copies, waits for them, and re-layouts: 16.7 us -> 2.03 us
    squeeze x2 -> x0, local copies, waits for them, and re-layouts: 1.52 us -> none  [the longest x1 0.76 us: fused(): routes[0]]
    pallas_call x1 -> x0, local copies, waits for them, and re-layouts: 1.15 us -> none  [fused(): pl.pallas_call(fused_kernel, out_shape=jax.ShapeDtypeStruct((t_tok, width...]
where the time goes in v2:
time: 63 us; the launch traced here: 62.8 us
  Pallas kernels  59.4 us (94%)
  local copies, waits for them, and re-layouts  3.34 us (5%)
    pallas_call x1, Pallas kernels, fused(): pl.pallas_call(fused_kernel, out_shape=jax.ShapeDtypeStruct((width, t_tok...  59.4 us
    unnamed x1, local copies, waits for them, and re-layouts  2.03 us
    reshape x1, local copies, waits for them, and re-layouts, fused(): gain.reshape(1, width)  1.31 us

profile of v2, /device:TPU:0, one launch (start us, length us, event | category | flops | bytes accessed | tf_op | source)
XLA Modules:
  0.0 62.8 jit_solution(4378574928792306369)
XLA Ops:
  0.0 1.3 %reshape.11.gain_ref = f32[1,2880]{1,0:T(1,128)} reshape(f32[2880]{0:T(1024)} %param.12) | data formatting | bytes 23040 | tf_op jit(solution)/shard_map/reshape | solution.py:314
  1.3 59.4 %shard_map.91 = bf16[2880,128]{1,0:T(8,128)(2,1)} custom-call(bf16[2880,128]{1,0:T(8,128)(2,1)} %bitcast.21, s32[1,128]{1,0:T(1,128)} %bitcast.24, f32[1,128]{1,0:T(1,128)} %bitcast.25, f32[1,2880]{1,0:T(1,128)} %reshape.11.gain_ref, s32[4,32]{1,0:T(4,128)} %bitcast.22, f32[4,32]{1,0:T(4,128)} %bitcast.23, bf16[720,2880]{1,0:T(8,128)(2,1)} %bitcast.17, ...), custom_call_target="tpu_custom_call" | custom-call | tf_op jit(solution)/shard_map/pallas_call | solution.py:282
  60.8 2.0 %copy.11 = bf16[128,2880]{0,1:T(8,128)(2,1)} copy(bf16[128,2880]{0,1:T(8,128)(2,1)} %bitcast.20) | data formatting | bytes 1474560

commit v3 on v2

--- a/solution.py
+++ b/solution.py
@@ -212,19 +212,23 @@
     gw = jnp.sum(jnp.where(g_lane == me, gb[...], 0.0), axis=3, keepdims=True)
     gw = gw.reshape(2 * n_e * HALF, 1)
     gate = acc_g[...]
-    hid[...] = ((acc_u[...] + 1.0) * gate * jax.nn.sigmoid(1.702 * gate) * gw).astype(bf16)
+    hid[...] = ((acc_u[...] + 1.0) * gate * jax.nn.sigmoid(1.702 * gate) * gw).astype(bf16).reshape(hid.shape)
     loads[3].wait()
 
+    def down_half(k, half):
+        start, w = chunks[k]
+        part = jnp.dot(hid[half], wd[:, start:start + w], preferred_element_type=f32)
+        ob[k, half, :, :, 0:w] = part.astype(bf16).reshape(n_e, HALF, w)
+
     def s_down(k):
-        start, w = chunks[k]
-        part = jnp.dot(hid[...], wd[:, start:start + w], preferred_element_type=f32).astype(bf16)
-        ob[k, :, :, :, 0:w] = part.reshape(2, n_e, HALF, w)
+        down_half(k, 1 - core)
         sends.append(send(
             ob.at[k, 1 - core, :, :, span[k]], rb.at[k, :, :, span[k]],
             d_s.at[k], d_r.at[k], {"expert": sibling},
         ))
 
     def s_pair(k):
+        down_half(k, core)
         arrived(rb.at[k, :, :, span[k]], d_r.at[k])
         sb[k] = (ob[k, core].astype(f32) + rb[k].astype(f32)).astype(bf16)
         rr[k, me] = sb[k, me]
@@ -296,7 +300,7 @@
             both,
             pltpu.VMEM((rows, hidden), f32),
             pltpu.VMEM((rows, hidden), f32),
-            pltpu.VMEM((rows, hidden), bf16),
+            pltpu.VMEM((2, rows // 2, hidden), bf16),
             both, block, block, block,
             single, line, line,
             dma((4,)), dma((n_z - 1,)), dma, dma((n_e - 1,)), dma,

time: 63 us -> 62.7 us (level)
  no operation moved by 1% of the time
where the time goes in v3:
time: 62.7 us; the launch traced here: 62.5 us
  Pallas kernels  59.1 us (94%)
  local copies, waits for them, and re-layouts  3.34 us (5%)
    pallas_call x1, Pallas kernels, fused(): pl.pallas_call(fused_kernel, out_shape=jax.ShapeDtypeStruct((width, t_tok...  59.1 us
    unnamed x1, local copies, waits for them, and re-layouts  2.03 us
    reshape x1, local copies, waits for them, and re-layouts, fused(): gain.reshape(1, width)  1.31 us

profile of v3, /device:TPU:0, one launch (start us, length us, event | category | flops | bytes accessed | tf_op | source)
XLA Modules:
  0.0 62.5 jit_solution(3850989326820111225)
XLA Ops:
  0.0 1.3 %reshape.11.gain_ref = f32[1,2880]{1,0:T(1,128)} reshape(f32[2880]{0:T(1024)} %param.12) | data formatting | bytes 23040 | tf_op jit(solution)/shard_map/reshape | solution.py:318
  1.3 59.1 %shard_map.91 = bf16[2880,128]{1,0:T(8,128)(2,1)} custom-call(bf16[2880,128]{1,0:T(8,128)(2,1)} %bitcast.21, s32[1,128]{1,0:T(1,128)} %bitcast.24, f32[1,128]{1,0:T(1,128)} %bitcast.25, f32[1,2880]{1,0:T(1,128)} %reshape.11.gain_ref, s32[4,32]{1,0:T(4,128)} %bitcast.22, f32[4,32]{1,0:T(4,128)} %bitcast.23, bf16[720,2880]{1,0:T(8,128)(2,1)} %bitcast.17, ...), custom_call_target="tpu_custom_call" | custom-call | tf_op jit(solution)/shard_map/pallas_call | solution.py:286
  60.5 2.0 %copy.11 = bf16[128,2880]{0,1:T(8,128)(2,1)} copy(bf16[128,2880]{0,1:T(8,128)(2,1)} %bitcast.20) | data formatting | bytes 1474560

commit v4 on v3

--- a/solution.py
+++ b/solution.py
@@ -5,7 +5,7 @@
 from jax.experimental.pallas import tpu as pltpu
 from jax.sharding import PartitionSpec as P
 
-CHUNK = 1536
+CHUNK = 1664
 LANES = 128
 HALF = 16
 NT = (((1,), (1,)), ((), ()))

time: 62.7 us -> 63.7 us (1.016)
  Pallas kernels: 59.1 us -> 60.1 us
    pallas_call x1, Pallas kernels: 59.1 us -> 60.1 us  [fused(): pl.pallas_call(fused_kernel, out_shape=jax.ShapeDtypeStruct((width, t_tok...]
where the time goes in v4:
time: 63.7 us; the launch traced here: 63.5 us
  Pallas kernels  60.1 us (94%)
  local copies, waits for them, and re-layouts  3.34 us (5%)
    pallas_call x1, Pallas kernels, fused(): pl.pallas_call(fused_kernel, out_shape=jax.ShapeDtypeStruct((width, t_tok...  60.1 us
    unnamed x1, local copies, waits for them, and re-layouts  2.03 us
    reshape x1, local copies, waits for them, and re-layouts, fused(): gain.reshape(1, width)  1.31 us

profile of v4, /device:TPU:0, one launch (start us, length us, event | category | flops | bytes accessed | tf_op | source)
XLA Modules:
  0.0 63.5 jit_solution(5840163819948627114)
XLA Ops:
  0.0 1.3 %reshape.11.gain_ref = f32[1,2880]{1,0:T(1,128)} reshape(f32[2880]{0:T(1024)} %param.12) | data formatting | bytes 23040 | tf_op jit(solution)/shard_map/reshape | solution.py:318
  1.3 60.1 %shard_map.91 = bf16[2880,128]{1,0:T(8,128)(2,1)} custom-call(bf16[2880,128]{1,0:T(8,128)(2,1)} %bitcast.21, s32[1,128]{1,0:T(1,128)} %bitcast.24, f32[1,128]{1,0:T(1,128)} %bitcast.25, f32[1,2880]{1,0:T(1,128)} %reshape.11.gain_ref, s32[4,32]{1,0:T(4,128)} %bitcast.22, f32[4,32]{1,0:T(4,128)} %bitcast.23, bf16[720,2880]{1,0:T(8,128)(2,1)} %bitcast.17, ...), custom_call_target="tpu_custom_call" | custom-call | tf_op jit(solution)/shard_map/pallas_call | solution.py:286
  61.4 2.0 %copy.11 = bf16[128,2880]{0,1:T(8,128)(2,1)} copy(bf16[128,2880]{0,1:T(8,128)(2,1)} %bitcast.20) | data formatting | bytes 1474560
